TPU v7x, 256 devices: a whole 4x4x8 slice. The times are simulated.
256 devices in a mesh: wide: 64 (over z, y, x_hi), narrow: 4 (over x_lo, core).
Axes of the slice: x: 4 (x_hi: 2, x_lo: 2; x = x_hi * 2 + x_lo), y: 4, z: 8, core: 2. Of those that a mesh axis runs over, the one named last changes fastest.
Arguments:
- embeddings: bfloat16 [32768, 4096], P(('wide', 'narrow')), may hold values from -6 to 6
- projection: bfloat16 [4096, 1024], P('wide'), as said below
- centroids: bfloat16 [8192, 1024], P('narrow'), as said below
- target: bfloat16 [32768, 8192], P('wide', 'narrow'), as said below
Outputs:
- grad_projected: float32 [32768, 1024], P(('wide', 'narrow'))
- grad_centroids: float32 [8192, 1024], P('narrow', 'wide')
- loss: float32 [], replicated
Inputs may be any that keep to these rules, and one draw needn't show every extreme that they name: Weights of each centroid row and projection are of the scale 1 / sqrt(1024) and 1 / sqrt(4194304). `target`: every entry is positive. `centroids`: finite values.
All inputs are finite; a program needn't handle non-finite values.
Results may differ from a plain program's by a relative error of at most 0.0065.
Values may be sent and summed in bfloat16 or wider, within the bound.
A program may use at most 64 MiB of HBM per device.

v0:
```python
import jax
import jax.numpy as jnp
from jax import lax
from jax.sharding import PartitionSpec as P

loss_scale = 64.0


def per_device(embeddings, projection, centroids, target):
    wide_count = lax.axis_size("wide")
    features = jnp.dot(
        embeddings,
        lax.all_gather(projection, "wide", axis=0, tiled=True),
        preferred_element_type=jnp.float32,
    ).astype(jnp.bfloat16)
    weights = target.astype(jnp.float32)
    wsum_local = jnp.sum(weights, axis=1)
    group = lax.all_gather(features, "narrow", axis=0, tiled=True)
    group_f = group.astype(jnp.float32)
    znorm = jnp.sum(group_f * group_f, axis=1)
    cnorm = jnp.einsum("kf,kf->k", centroids, centroids, preferred_element_type=jnp.float32)
    inner = lax.dot_general(
        group, centroids, (((1,), (1,)), ((), ())), preferred_element_type=jnp.float32
    )
    dist = znorm[:, None] + cnorm[None, :] - 2.0 * inner
    kernel = 1.0 / (1.0 + dist)
    ksum_local = jnp.sum(kernel, axis=1)
    cross_local = jnp.sum(weights * (jnp.log(weights) + jnp.log(1.0 + dist)), axis=1)
    wsum, ksum, cross = lax.psum((wsum_local, ksum_local, cross_local), "narrow")
    row_loss = cross / wsum - jnp.log(wsum) + jnp.log(ksum)
    loss_sum = lax.psum(jnp.sum(row_loss), "wide")
    loss = loss_sum / (group.shape[0] * wide_count)
    coeff = (loss_scale * kernel * (weights / wsum[:, None] - kernel / ksum[:, None])).astype(
        jnp.bfloat16
    )
    rowg = jnp.sum(coeff, axis=1, dtype=jnp.float32)
    pull = jnp.dot(coeff, centroids, preferred_element_type=jnp.float32)
    doc_part = 2.0 * (rowg[:, None] * group_f - pull)
    grad_projected = lax.psum_scatter(doc_part, "narrow", scatter_dimension=0, tiled=True)
    colg = jnp.sum(coeff, axis=0, dtype=jnp.float32)
    push = lax.dot_general(
        coeff, group, (((0,), (0,)), ((), ())), preferred_element_type=jnp.float32
    )
    cent_part = -2.0 * (push - colg[:, None] * centroids.astype(jnp.float32))
    grad_centroids = lax.psum_scatter(cent_part, "wide", scatter_dimension=1, tiled=True)
    return (grad_projected, grad_centroids, loss)


def solution(mesh):
    placed = (P(("wide", "narrow"), None), P("wide", None), P("narrow", None), P("wide", "narrow"))
    return jax.shard_map(
        per_device,
        mesh=mesh,
        in_specs=placed,
        out_specs=(P(("wide", "narrow"), None), P("narrow", "wide"), P()),
        check_vma=False,
    )
```

profile of v0, /device:TPU:8, one launch (start us, length us, event | category | flops | bytes accessed | tf_op | source)
XLA Modules:
  0.0 637.4 jit_solution(3865384294239850562)
XLA Ops:
  7.2 0.0 copy-start
  7.2 0.0 all-gather.3.cloned.1.call-start
  7.2 0.7 all-gather.3.cloned.1.call-update
  7.9 0.0 all-gather.5.cloned.1.call-start
  8.0 157.1 %all-gather.3.cloned.1.call-done = bf16[4096,1024]{1,0:T(8,128)(2,1)} async-done(((bf16[64,1024]{1,0:T(8,128)(2,1)}), bf16[4096,1024]{1,0:T(8,128)(2,1)}) %all-gather.3.cloned.1.call-update) | async-done | bytes 8388624 | tf_op jit(solution)/shard_map/all_gather | solution.py:13
  165.1 0.0 copy-done
  165.1 5.3 convolution_convert_fusion
  170.4 0.0 all-gather.5.cloned.1.call-update
  170.5 0.0 reduce-scatter.3.cloned.1.call-start
  170.5 3.2 fusion
  173.7 17.0 %all-gather.5.cloned.1.call-done = bf16[512,1024]{1,0:T(8,128)(2,1)} async-done(((bf16[128,1024]{1,0:T(8,128)(2,1)}), bf16[512,1024]{1,0:T(8,128)(2,1)}) %all-gather.5.cloned.1.call-update) | async-done | bytes 1048592 | tf_op jit(solution)/shard_map/all_gather | solution.py:18
  190.7 1.5 fusion.6
  192.2 0.0 copy-done.2
  192.2 8.1 %fusion.5 = (f32[512]{0:T(512)S(1)}, f32[512]{0:T(512)S(1)}, f32[512]{0:T(512)S(1)}, f32[512,2048]{1,0:T(8,128)}) fusion(bf16[512,2048]{1,0:T(8,128)(2,1)S(1)} %copy-done.2, bf16[512,1024]{1,0:T(8,128)(2,1)} %all-gather.5.cloned.1.call-done, bf16[2048,1024]{1,0:T(8,128)(2,1)} %param.6, f32[2048]{0:T(1024)S(1)} %fusion, f32[512]{0:T(512)S(1)} %fusion.6), kind=kOutput, calls=%fused_computation.13 | convolution fusion | flops 2159016448 | bytes 11550720 | tf_op jit(solution)/shard_map/dot_general | solution.py:22
  200.3 6.5 %all-reduce = (f32[512]{0:T(512)S(1)}, f32[512]{0:T(512)S(1)}, f32[512]{0:T(512)S(1)}) all-reduce(f32[512]{0:T(512)S(1)} %get-tuple-element.4, f32[512]{0:T(512)S(1)} %get-tuple-element.5, f32[512]{0:T(512)S(1)} %get-tuple-element.3), channel_id=1, replica_groups=mesh['wide'=64,'narrow'=4] {'narrow'}, use_global_device_ids=true, to_apply=%region_4.0 | all-reduce | flops 1536 | bytes 12288 | tf_op jit(solution)/shard_map/psum | solution.py:29
  206.8 0.0 copy-start.1
  206.8 0.0 copy-start.5
  206.8 3.8 convert_reduce_fusion.1
  210.7 0.0 copy-start.3
  210.7 1.3 copy-done.3
  212.0 0.0 copy-done.1
  212.0 0.0 copy-done.5
  212.0 3.7 fusion.8
  215.8 0.0 reduce-scatter.3.cloned.1.call-update
  215.8 0.2 reduce-scatter.5.cloned.1.call-start
  216.0 6.6 %copy.7 = bf16[2048,1024]{0,1:T(8,128)(2,1)} copy(bf16[2048,1024]{1,0:T(8,128)(2,1)} %param.6) | data formatting | bytes 8388608 | tf_op args[2]
  222.6 8.4 %subtract_multiply_fusion = f32[2048,1024]{0,1:T(8,128)} fusion(bf16[2048,1024]{0,1:T(8,128)(2,1)} %copy.7, f32[2048]{0:T(1024)S(1)} %get-tuple-element.6, bf16[512,2048]{1,0:T(8,128)(2,1)S(1)} %copy-done.4, bf16[512,1024]{1,0:T(8,128)(2,1)} %all-gather.5.cloned.1.call-done), kind=kOutput, calls=%fused_computation.2 | convolution fusion | flops 2155872256 | bytes 15736832 | tf_op jit(solution)/shard_map/dot_general | solution.py:41
  231.0 0.0 reduce-scatter.5.cloned.1.call-update
  231.1 0.6 add_reduce_fusion
  231.7 180.6 %psum.31 = f32[]{:T(128)} all-reduce(f32[]{:T(128)} %add_reduce_fusion), channel_id=1, replica_groups=mesh['wide'=64,'narrow'=4] {'wide'}, use_global_device_ids=true, to_apply=%region_12.0 | all-reduce | flops 1 | bytes 8 | tf_op jit(solution)/shard_map/psum | solution.py:31
  412.9 0.0 reduce-scatter.3.cloned.1.call-done
  412.9 216.8 %reduce-scatter.5.cloned.1.call-done = f32[2048,16]{0,1:T(8,128)} async-done(((f32[2048,1024]{0,1:T(8,128)}), f32[2048,16]{0,1:T(8,128)}) %reduce-scatter.5.cloned.1.call-update) | async-done | bytes 131088 | tf_op jit(solution)/shard_map/reduce_scatter | solution.py:45
  (3 shorter events, 0.0 us)
Async XLA Ops:
  7.2 157.9 %copy-start = (bf16[128,4096]{1,0:T(8,128)(2,1)S(1)}, bf16[128,4096]{1,0:T(8,128)(2,1)}, u32[]{:S(2)}) copy-start(bf16[128,4096]{1,0:T(8,128)(2,1)} %param.4) | copy-start | bytes 3145732
  7.2 157.9 %all-gather.3.cloned.1.call-start = ((), (), s32[]{:S(2)}) async-start(), calls=%async_computation.2 | async-start | bytes 8519680 | tf_op jit(solution)/shard_map/all_gather | solution.py:13
  7.9 182.8 %all-gather.5.cloned.1.call-start = ((), (), s32[]{:S(2)}) async-start(), calls=%async_computation.3 | async-start | bytes 1310720 | tf_op jit(solution)/shard_map/all_gather | solution.py:18
  170.4 21.8 %copy-start.2 = (bf16[512,2048]{1,0:T(8,128)(2,1)S(1)}, bf16[512,2048]{1,0:T(8,128)(2,1)}, u32[]{:S(2)}) copy-start(bf16[512,2048]{1,0:T(8,128)(2,1)} %param.7) | copy-start | bytes 6291460
  170.5 242.5 %reduce-scatter.3.cloned.1.call-start = ((), (), s32[]{:S(2)}) async-start(), calls=%async_computation.4 | async-start | bytes 2621440 | tf_op jit(solution)/shard_map/reduce_scatter | solution.py:39
  206.8 5.2 copy-start.1
  206.8 5.2 copy-start.5
  210.7 1.4 copy-start.3
  215.8 6.8 %copy-start.4 = (bf16[512,2048]{1,0:T(8,128)(2,1)S(1)}, bf16[512,2048]{1,0:T(8,128)(2,1)}, u32[]{:S(2)}) copy-start(bf16[512,2048]{1,0:T(8,128)(2,1)} %copy-done.3) | copy-start | bytes 6291460
  215.8 413.9 %reduce-scatter.5.cloned.1.call-start = ((), (), s32[]{:S(2)}) async-start(), calls=%async_computation.5 | async-start | bytes 8519680 | tf_op jit(solution)/shard_map/reduce_scatter | solution.py:45
Sparse Core Ops, SparseCore 0:
  11.5 153.5 all-gather.2
  170.6 20.0 all-gather.4
  215.9 32.1 reduce-scatter.2
  251.2 378.4 reduce-scatter.4
where the time goes:
time: 640 us; the launch traced here: 637 us
  waiting for transfers between devices  392 us (61%)
  blocking collectives  187 us (29%)
  matrix products  25.6 us (4%)
  between operations  15.6 us (2%)
  other arithmetic  9.13 us (1%)
  local copies, waits for them, and re-layouts  7.96 us (1%)
    reduce_scatter x1, waiting for transfers between devices, per_device(): lax.psum_scatter(cent_part, 'wide', scatter_dimension=1, tiled=True)  217 us
    psum x1, blocking collectives, per_device(): loss_sum = lax.psum(jnp.sum(row_loss), 'wide')  181 us
    all_gather x1, waiting for transfers between devices, per_device(): lax.all_gather(projection, 'wide', axis=0, tiled=True)  157 us
    all_gather x1, waiting for transfers between devices, per_device(): group = lax.all_gather(features, 'narrow', axis=0, tiled=True)  17 us
  transfers between devices with their start and end apart: 4, of which 3 were waited for; matrix products, arithmetic and copies ran while one was open for 3% of the time, Pallas kernels for 0%

commit v1 on v0

v1 whole, which is shorter than its diff:
```python
import jax
import jax.numpy as jnp
from jax import lax
from jax.experimental import pallas as pl
from jax.experimental.pallas import tpu as pltpu
from jax.sharding import PartitionSpec as P

NZ, NY, NX = 8, 4, 4
DIN, DZ, HALF = 4096, 1024, 512
DOCS_DEV, CHIP_DOCS, RING_DOCS = 128, 256, 1024
CENTS = 1024
DOCS = 32768
SCALE = 64.0
ROWS_B = 48
ROWS_A = 80
A_PLUS = 48
ORDER = (4, 3, -3, 2, -2, 1, -1, 0)
N_SEM = 160
bf16, f32 = jnp.bfloat16, jnp.float32


def body(
    emb, proj, cent, target,
    gp_ref, gc_ref, loss_ref,
    pbuf, ebuf, cbuf, ct, tbuf, feat, ft, kbuf, cbf, stats, ab, rowg_ref, cn_ref, colg_ref,
    rs, rfwd, rone, rcomb, csend, zsend, zrecv, ysum, xsend, xrecv,
    psend, pown, precv, gsend, gx, ly, lz,
    send_sems, recv_sems, local_sems,
):
    wide, narrow = lax.axis_index("wide"), lax.axis_index("narrow")
    z, y, xh = wide // 8, (wide // 2) % 4, wide % 2
    xl, core = narrow // 2, narrow % 2
    x = xh * 2 + xl

    def device(dx=0, dy=0, dz=0, dc=0):
        tx, ty, tz, tc = (x + dx + NX) % NX, (y + dy + NY) % NY, (z + dz + NZ) % NZ, (core + dc) % 2
        return (tz * 8 + ty * 2 + tx // 2, (tx % 2) * 2 + tc)

    def to_device(tx):
        return (z * 8 + y * 2 + tx // 2, (tx % 2) * 2 + core)

    def zi(dz):
        return (z + dz + NZ) % NZ

    def yi(dy):
        return (y + dy + NY) % NY

    def xi(dx):
        return (x + dx + NX) % NX

    copies = []

    def send(src, dst, target_device):
        number = len(copies)
        copy = pltpu.make_async_remote_copy(
            src_ref=src, dst_ref=dst, send_sem=send_sems.at[number], recv_sem=recv_sems.at[number],
            device_id=target_device, device_id_type=pl.DeviceIdType.MESH,
        )
        copy.start()
        copies.append(copy)
        return copy

    locals_ = []

    def local(src, dst):
        copy = pltpu.make_async_copy(src, dst, local_sems.at[len(locals_)])
        copy.start()
        locals_.append(copy)
        return copy

    own_rows = pl.ds(pl.multiple_of(xh * 64, 64), 64)
    own_cols = pl.ds(pl.multiple_of(core * HALF, HALF), HALF)
    l_proj = local(proj.at[:, own_cols], pbuf.at[z, y, own_rows])
    l_emb = local(emb, ebuf.at[pl.ds(pl.multiple_of(core * 128, 128), 128)])
    j_rows = pl.ds(pl.multiple_of(xh * CENTS, CENTS), CENTS)
    other_rows = pl.ds(pl.multiple_of((1 - xh) * CENTS, CENTS), CENTS)
    my_docs = pl.ds(pl.multiple_of(xh * 512, 512), 512)
    l_cent = local(cent.at[j_rows], cbuf)
    l_tgt = local(target.at[:, j_rows], tbuf.at[my_docs])

    ring = [(dx, dc) for dx in range(NX) for dc in range(2) if (dx, dc) != (0, 0)]
    peers = [device(dx=dx, dc=dc) for dx, dc in ring]
    peers += [device(dz=d) for d in range(1, NZ)] + [device(dy=d) for d in range(1, NY)]
    barrier = pltpu.get_barrier_semaphore()
    for peer in peers:
        pl.semaphore_signal(barrier, inc=1, device_id=peer, device_id_type=pl.DeviceIdType.MESH)
    pl.semaphore_wait(barrier, len(peers))

    a_start = pl.multiple_of((1 - xh) * 48, 16)
    b_start = pl.multiple_of(xh * 80, 16)

    def rows_of(part):
        if part == "a":
            return pl.ds(a_start, ROWS_A)
        if part == "a+":
            return pl.ds(a_start, A_PLUS)
        if part == "a-":
            return pl.ds(pl.multiple_of(a_start + A_PLUS, 16), ROWS_A - A_PLUS)
        return pl.ds(b_start, ROWS_B)

    def move(part, at_z, at_y, **hop):
        where = pbuf.at[zi(at_z), yi(at_y), rows_of(part)]
        return send(where, where, device(**hop))

    bz, az, ay, by = {}, {}, {}, {}

    def b_start_chain(q):
        bz[q, 1, 1] = move("b", 0, q, dz=1)
        bz[q, -1, 1] = move("b", 0, q, dz=-1)

    l_proj.wait()
    where = pbuf.at[z, y, own_rows]
    b_start_chain(0)
    for hop in (1, -1, 2):
        by[hop] = move("b", 0, 0, dy=hop)
    x_swap = send(where, where, to_device(3 - x))
    l_emb.wait()
    mine = ebuf.at[pl.ds(pl.multiple_of(core * 128, 128), 128)]
    e_copy = send(mine, mine, device(dc=1))
    l_tgt.wait()
    t_copy = send(target.at[:, other_rows], tbuf.at[my_docs], device(dx=2))

    x_swap.wait_recv()

    def a_y_sends(dz):
        ay[dz, 1] = move("a", dz, 0, dy=1)
        ay[dz, -1] = move("a", dz, 0, dy=-1)

    def a_y_forward(dz):
        if dz % 2 == 0:
            ay[dz, 1].wait_recv()
            ay[dz, 2] = move("a", dz, -1, dy=1)
        else:
            ay[dz, -1].wait_recv()
            ay[dz, 2] = move("a", dz, 1, dy=-1)

    az[1, 1] = move("a", 0, 0, dz=1)
    az[-1, 1] = move("a", 0, 0, dz=-1)
    a_y_sends(0)
    by[1].wait_recv()
    b_start_chain(-1)
    by[-1].wait_recv()
    b_start_chain(1)
    by[2].wait_recv()
    b_start_chain(2)

    def b_step(step, q):
        for sign in (1, -1):
            if (q, sign, step) in bz:
                bz[q, sign, step].wait_recv()
                if step < 3 or (step == 3 and (sign == 1) == (q in (0, 2))):
                    bz[q, sign, step + 1] = move("b", -sign * step, q, dz=sign)

    def a_step(step):
        for sign in (1, -1):
            az[sign, step].wait_recv()
            if step < 3:
                az[sign, step + 1] = move("a", -sign * step, 0, dz=sign)
            elif step == 3:
                az[sign, 4] = move("a+" if sign == 1 else "a-", -sign * step, 0, dz=sign)
        if step < 4:
            a_y_sends(step)
            a_y_sends(-step)
        else:
            a_y_sends(4)

    def target_stats(block):
        rows = pl.ds(pl.multiple_of(block * 128, 128), 128)
        wp = jnp.zeros((128, 128), f32)
        lp = jnp.zeros((128, 128), f32)
        for lane in range(8):
            t = tbuf[rows, lane * 128:(lane + 1) * 128].astype(f32)
            wp = wp + t
            lp = lp + t * jnp.log(t)
        stats[me8, 0:1, rows] = jnp.sum(wp.T, axis=0, keepdims=True)
        stats[me8, 1:2, rows] = jnp.sum(lp.T, axis=0, keepdims=True)

    me8 = x * 2 + core
    stats[me8] = jnp.zeros((8, RING_DOCS), f32)

    def centroid_block(j):
        cols = pl.ds(pl.multiple_of(j * 128, 128), 128)
        c = cbuf[cols, :].astype(f32).T
        ct[:, cols] = c.astype(bf16)
        cn_ref[0:1, cols] = jnp.sum(c * c, axis=0, keepdims=True)

    l_cent.wait()
    for step in (1, 2, 3, 4):
        b_step(step, 0)
        a_step(step)
        for q in (-1, 1, 2):
            b_step(step, q)
        if step == 1:
            a_y_forward(0)
        else:
            a_y_forward(step - 1)
            a_y_forward(-(step - 1))
        centroid_block(2 * step - 2)
        centroid_block(2 * step - 1)
        target_stats(xh * 4 + step - 1)
    a_y_forward(4)
    t_copy.wait_recv()

    @pl.loop(0, 4)
    def _(i):
        target_stats((1 - xh) * 4 + i)

    e_copy.wait_recv()
    for dz in (0, 1, -1, 2, -2, 3, -3, 4):
        ay[dz, -1 if dz % 2 == 0 else 1].wait_recv()
        ay[dz, 2].wait_recv()

    def chip_rows(dx):
        return pl.ds(pl.multiple_of(xi(dx) * CHIP_DOCS, CHIP_DOCS), CHIP_DOCS)

    own = jnp.dot(ebuf[...], pbuf[...].reshape(DIN, HALF), preferred_element_type=f32).astype(bf16)
    feat[core, chip_rows(0), :] = own
    fx = {}

    def feat_send(at_x, **hop):
        where = feat.at[core, chip_rows(at_x)]
        return send(where, where, device(**hop))

    fx[1] = feat_send(0, dx=1)
    fx[3] = feat_send(0, dx=-1)
    fc = {0: feat_send(0, dc=1)}
    fx[2] = feat_send(0, dx=2)

    def inner(dx):
        fc[dx].wait_recv()
        rows = chip_rows(dx)
        f0, f1 = feat[0, rows, :], feat[1, rows, :]
        g = jnp.dot(f0, ct[0:HALF, :], preferred_element_type=f32)
        g = g + jnp.dot(f1, ct[HALF:DZ, :], preferred_element_type=f32)
        g0, g1 = f0.astype(f32), f1.astype(f32)
        zn = 1.0 + jnp.sum(g0 * g0 + g1 * g1, axis=1, keepdims=True)
        kp = jnp.zeros((CHIP_DOCS, 128), f32)
        cp = jnp.zeros((CHIP_DOCS, 128), f32)
        for lane in range(8):
            cols = slice(lane * 128, (lane + 1) * 128)
            u = (zn + cn_ref[0:1, cols]) - 2.0 * g[:, cols]
            r = pl.reciprocal(u, approx=True)
            k = r * (2.0 - u * r)
            kbuf[rows, cols] = k
            kp = kp + k
            cp = cp + tbuf[rows, cols].astype(f32) * jnp.log(u)
        stats[me8, 2:3, rows] = jnp.sum(kp.T, axis=0, keepdims=True)
        stats[me8, 3:4, rows] = jnp.sum(cp.T, axis=0, keepdims=True)

    def transpose_features(dx):
        rows = chip_rows(dx)
        ft[0:HALF, rows] = feat[0, rows, :].astype(f32).T.astype(bf16)
        ft[HALF:DZ, rows] = feat[1, rows, :].astype(f32).T.astype(bf16)

    inner(0)
    transpose_features(0)
    for dx in (1, 3, 2):
        fx[dx].wait_recv()
        fc[NX - dx] = feat_send(NX - dx, dc=1)
        inner(NX - dx)
        if dx != 2:
            transpose_features(NX - dx)

    st = []
    for dx, dc in ring:
        st.append(send(stats.at[me8], stats.at[me8], device(dx=dx, dc=dc)))
    transpose_features(2)
    for copy in st:
        copy.wait_recv()
    tot = stats[0]
    for i in range(1, 8):
        tot = tot + stats[i]
    wsum, tlog, ksum, clog = tot[0:1], tot[1:2], tot[2:3], tot[3:4]
    row_loss = (tlog + clog) / wsum - jnp.log(wsum) + jnp.log(ksum)
    ly[y] = jnp.broadcast_to(jnp.sum(row_loss, axis=1, keepdims=True), (8, 128))
    lsy = [send(ly.at[y], ly.at[y], device(dy=d)) for d in range(1, NY)]
    ra, rb = SCALE / wsum, SCALE / ksum
    for block in range(8):
        rows = slice(block * 128, (block + 1) * 128)
        ab[0, rows, :] = jnp.broadcast_to(ra[:, rows], (128, 128)).T
        ab[1, rows, :] = jnp.broadcast_to(rb[:, rows], (128, 128)).T

    colg_ref[...] = jnp.zeros((8, CENTS), f32)

    @pl.loop(0, 8)
    def _(block):
        rows = pl.ds(pl.multiple_of(block * 128, 128), 128)
        a, b = ab[0, rows, :], ab[1, rows, :]
        rp = jnp.zeros((128, 128), f32)
        for lane in range(8):
            cols = slice(lane * 128, (lane + 1) * 128)
            k = kbuf[rows, cols]
            cf = (k * (tbuf[rows, cols].astype(f32) * a - k * b)).astype(bf16)
            cbf[rows, cols] = cf
            cf = cf.astype(f32)
            rp = rp + cf
            colg_ref[:, cols] += jnp.sum(cf.reshape(16, 8, 128), axis=0)
        rowg_ref[rows, :] = jnp.broadcast_to(jnp.sum(rp, axis=1, keepdims=True), (128, 128))

    colg = jnp.sum(colg_ref[...], axis=0, keepdims=True)
    fwd, one, comb, zs = {}, {}, {}, {}

    def push_pair(first):
        rows = [pl.ds(pl.multiple_of(zi(ORDER[i]) * 128, 128), 128) for i in (first, first + 1)]
        lhs = jnp.concatenate([ft[r, :] for r in rows], axis=0)
        prod = jnp.dot(lhs, cbf[...], preferred_element_type=f32)
        for k, i in enumerate((first, first + 1)):
            part = prod[k * 128:(k + 1) * 128]
            part = -2.0 * (part - colg * ct[rows[k], :].astype(f32))
            rs[i] = part.astype(bf16).reshape(4, 32, CENTS)
            sign = 1 if i % 2 == 0 else -1
            fwd[i] = send(rs.at[i, yi(2)], rfwd.at[i], device(dy=sign))
            one[i] = send(rs.at[i, yi(-sign)], rone.at[i], device(dy=-sign))

    def combine(i):
        sign = 1 if i % 2 == 0 else -1
        fwd[i].wait_recv()
        csend[i] = (rs[i, yi(sign)].astype(f32) + rfwd[i].astype(f32)).astype(bf16)
        comb[i] = send(csend.at[i], rcomb.at[i], device(dy=sign))

    def y_total(i):
        one[i].wait_recv()
        comb[i].wait_recv()
        total = rs[i, y].astype(f32) + rone[i].astype(f32) + rcomb[i].astype(f32)
        if ORDER[i] == 0:
            ysum[...] = total
        else:
            zsend[i] = total.astype(bf16)
            zs[i] = send(zsend.at[i], zrecv.at[i], device(dz=ORDER[i]))

    def pull_block(dx):
        rows = chip_rows(dx)
        pull = jnp.dot(cbf[rows, :], cbuf[...], preferred_element_type=f32)
        rg = rowg_ref[rows, :]
        blocks = []
        for h in range(2):
            f = feat[h, rows, :].astype(f32)
            rgw = jnp.concatenate([rg] * 4, axis=1)
            blocks.append(2.0 * (rgw * f - pull[:, h * HALF:(h + 1) * HALF]))
        part = jnp.concatenate(blocks, axis=1)
        psend[dx % NX, 0] = part[0:128].astype(bf16)
        psend[dx % NX, 1] = part[128:256].astype(bf16)
        return send(psend.at[dx % NX, 1 - core], precv.at[dx % NX], device(dc=1))

    pulls, gs = {}, {}

    def pull_sum(dx):
        pulls[dx].wait_recv()
        both = psend[dx, core].astype(f32) + precv[dx].astype(f32)
        if dx == 0:
            pown[...] = both
        else:
            gsend[dx - 1] = both.astype(bf16)
            gs[dx] = send(gsend.at[dx - 1], gx.at[dx - 1], device(dx=dx))

    push_pair(0)
    push_pair(2)
    push_pair(4)
    push_pair(6)
    combine(0)
    pulls[2] = pull_block(2)
    combine(1)
    pulls[1] = pull_block(1)
    combine(2)
    pull_sum(2)
    pulls[3] = pull_block(3)
    combine(3)
    pull_sum(1)
    pulls[0] = pull_block(0)
    pull_sum(3)
    combine(4)
    pull_sum(0)
    for copy in lsy:
        copy.wait_recv()
    lz[z] = (ly[0] + ly[1]) + (ly[2] + ly[3])
    lsz = [send(lz.at[z], lz.at[z], device(dz=d)) for d in range(1, NZ)]
    combine(5)
    combine(6)
    combine(7)
    for i in range(8):
        y_total(i)
    for dx in (1, 3, 2):
        gs[dx].wait_recv()
    gp_ref[...] = pown[...] + gx[0].astype(f32) + gx[1].astype(f32) + gx[2].astype(f32)
    for copy in lsz:
        copy.wait_recv()
    total = lz[0]
    for i in range(1, NZ):
        total = total + lz[i]
    loss_ref[...] = total * (1.0 / DOCS)
    for i in range(7):
        zs[i].wait_recv()
    for h in range(2):
        rows = slice(h * 16, (h + 1) * 16)
        part = ysum[rows, :]
        for i in range(7):
            part = part + zrecv[i, rows, :].astype(f32)
        ysum[rows, :] = part
    xsend[...] = ysum[pl.ds(pl.multiple_of((1 - xh) * 16, 16), 16), :].astype(bf16)
    last = send(xsend, xrecv, device(dx=2))
    gc_ref[:, j_rows] = ysum[pl.ds(pl.multiple_of(xh * 16, 16), 16), :]
    last.wait_recv()
    gc_ref[:, other_rows] = xrecv[...].astype(f32)
    for copy in copies:
        copy.wait_send()


def per_device(embeddings, projection, centroids, target):
    vmem = pltpu.VMEM
    gp, gct, loss = pl.pallas_call(
        body,
        name="cluster_head",
        out_shape=(
            jax.ShapeDtypeStruct((DOCS_DEV, DZ), f32),
            jax.ShapeDtypeStruct((16, 2 * CENTS), f32),
            jax.ShapeDtypeStruct((8, 128), f32),
        ),
        in_specs=[pl.BlockSpec(memory_space=pl.ANY)] * 4,
        out_specs=(pl.BlockSpec(memory_space=vmem),) * 3,
        scratch_shapes=[
            vmem((NZ, NY, 128, HALF), bf16),
            vmem((CHIP_DOCS, DIN), bf16),
            vmem((CENTS, DZ), bf16),
            vmem((DZ, CENTS), bf16),
            vmem((RING_DOCS, CENTS), bf16),
            vmem((2, RING_DOCS, HALF), bf16),
            vmem((DZ, RING_DOCS), bf16),
            vmem((RING_DOCS, CENTS), f32),
            vmem((RING_DOCS, CENTS), bf16),
            vmem((8, 8, RING_DOCS), f32),
            vmem((2, RING_DOCS, 128), f32),
            vmem((RING_DOCS, 128), f32),
            vmem((8, CENTS), f32),
            vmem((8, CENTS), f32),
            vmem((8, 4, 32, CENTS), bf16),
            vmem((8, 32, CENTS), bf16),
            vmem((8, 32, CENTS), bf16),
            vmem((8, 32, CENTS), bf16),
            vmem((8, 32, CENTS), bf16),
            vmem((7, 32, CENTS), bf16),
            vmem((7, 32, CENTS), bf16),
            vmem((32, CENTS), f32),
            vmem((16, CENTS), bf16),
            vmem((16, CENTS), bf16),
            vmem((4, 2, 128, DZ), bf16),
            vmem((128, DZ), f32),
            vmem((4, 128, DZ), bf16),
            vmem((3, 128, DZ), bf16),
            vmem((3, 128, DZ), bf16),
            vmem((NY, 8, 128), f32),
            vmem((NZ, 8, 128), f32),
            pltpu.SemaphoreType.DMA((N_SEM,)),
            pltpu.SemaphoreType.DMA((N_SEM,)),
            pltpu.SemaphoreType.DMA((4,)),
        ],
        compiler_params=pltpu.CompilerParams(
            collective_id=0, has_side_effects=True, vmem_limit_bytes=60 * 2**20
        ),
        cost_estimate=pl.CostEstimate(flops=7_500_000_000, bytes_accessed=9_000_000, transcendentals=3_000_000),
    )(embeddings, projection, centroids, target)
    return gp, gct.T, loss[0, 0]


def solution(mesh):
    placed = (P(("wide", "narrow"), None), P("wide", None), P("narrow", None), P("wide", "narrow"))
    return jax.shard_map(
        per_device,
        mesh=mesh,
        in_specs=placed,
        out_specs=(P(("wide", "narrow"), None), P("narrow", "wide"), P()),
        check_vma=False,
    )
```

time: 640 us -> 132 us (0.21)
  waiting for transfers between devices: 392 us -> 0 us
  blocking collectives: 187 us -> 0 us
  Pallas kernels: 0 us -> 125 us
  matrix products: 25.6 us -> 0 us
  between operations: 15.6 us -> 0.64 us
  other arithmetic: 9.13 us -> 0 us
    reduce_scatter x2 -> x0, waiting for transfers between devices: 217 us -> none  [the longest x1 217 us: per_device(): lax.psum_scatter(cent_part, 'wide', scatter_dimension=1, tiled=True)]
    psum x2 -> x0, blocking collectives: 187 us -> none  [the longest x1 181 us: per_device(): loss_sum = lax.psum(jnp.sum(row_loss), 'wide')]
    all_gather x2 -> x0, waiting for transfers between devices: 174 us -> none  [the longest x1 157 us: per_device(): lax.all_gather(projection, 'wide', axis=0, tiled=True)]
    pallas_call x0 -> x1, Pallas kernels: none -> 125 us  [per_device(): pl.pallas_call(body, name='cluster_head', out_shape=(jax.ShapeDtypeStruct...]
    dot_general x4 -> x0, matrix products: 25.6 us -> none  [the longest x1 8.44 us: per_device(): lax.dot_general(coeff, group, (((0,), (0,)), ((), ())), preferred_element...]
  transfers between devices with their start and end apart: 4 -> 0, of which waited for: 3 -> 0; matrix products, arithmetic and copies ran while one was open for 3% -> 0% of each run, Pallas kernels for 0% -> 0%
where the time goes in v1:
time: 132 us; the launch traced here: 130 us
  Pallas kernels  125 us (95%)
  local copies, waits for them, and re-layouts  4.65 us (4%)
    pallas_call x1, Pallas kernels, per_device(): pl.pallas_call(body, name='cluster_head', out_shape=(jax.ShapeDtypeStruct...  125 us
    unnamed x2, local copies, waits for them, and re-layouts  3.45 us

profile of v1, /device:TPU:8, one launch (start us, length us, event | category | flops | bytes accessed | tf_op | source)
XLA Modules:
  0.0 130.1 jit_solution(10980252116331322095)
XLA Ops:
  0.6 124.8 %cluster_head.1 = (f32[128,1024]{1,0:T(8,128)}, f32[16,2048]{1,0:T(8,128)}, f32[8,128]{1,0:T(8,128)}) custom-call(bf16[128,4096]{1,0:T(8,128)(2,1)} %emb.1, bf16[64,1024]{1,0:T(8,128)(2,1)} %proj.1, bf16[2048,1024]{1,0:T(8,128)(2,1)} %cent.1, bf16[512,2048]{1,0:T(8,128)(2,1)} %target.1), custom_call_target="tpu_custom_call" | custom-call | flops 7500000256 | bytes 9000000 | tf_op jit(solution)/shard_map/cluster_head/pallas_call | solution.py:410
  125.4 1.2 slice.3
  126.6 1.9 %copy.9 = f32[128,1024]{1,0:T(8,128)} copy(f32[128,1024]{1,0:T(8,128)} %get-tuple-element.12) | data formatting | bytes 1048576
  128.5 1.6 %copy.10 = f32[2048,16]{0,1:T(8,128)} copy(f32[2048,16]{0,1:T(8,128)} %bitcast.2) | data formatting | bytes 262144

commit v2 on v1

--- a/solution.py
+++ b/solution.py
@@ -11,9 +11,6 @@
 CENTS = 1024
 DOCS = 32768
 SCALE = 64.0
-ROWS_B = 48
-ROWS_A = 80
-A_PLUS = 48
 ORDER = (4, 3, -3, 2, -2, 1, -1, 0)
 N_SEM = 160
 bf16, f32 = jnp.bfloat16, jnp.float32
@@ -86,41 +83,33 @@
         pl.semaphore_signal(barrier, inc=1, device_id=peer, device_id_type=pl.DeviceIdType.MESH)
     pl.semaphore_wait(barrier, len(peers))
 
-    a_start = pl.multiple_of((1 - xh) * 48, 16)
-    b_start = pl.multiple_of(xh * 80, 16)
-
-    def rows_of(part):
-        if part == "a":
-            return pl.ds(a_start, ROWS_A)
-        if part == "a+":
-            return pl.ds(a_start, A_PLUS)
-        if part == "a-":
-            return pl.ds(pl.multiple_of(a_start + A_PLUS, 16), ROWS_A - A_PLUS)
-        return pl.ds(b_start, ROWS_B)
+    other_half = pl.ds(pl.multiple_of((1 - xh) * 64, 64), 64)
 
     def move(part, at_z, at_y, **hop):
-        where = pbuf.at[zi(at_z), yi(at_y), rows_of(part)]
+        where = pbuf.at[zi(at_z), yi(at_y), own_rows if part == "a" else other_half]
         return send(where, where, device(**hop))
 
+    def move_half(half, at_z, **hop):
+        start = pl.multiple_of(xh * 64 + half * 32, 32)
+        where = pbuf.at[zi(at_z), y, pl.ds(start, 32)]
+        return send(where, where, device(**hop))
+
     bz, az, ay, by = {}, {}, {}, {}
 
-    def b_start_chain(q):
+    def b_own(q):
         bz[q, 1, 1] = move("b", 0, q, dz=1)
         bz[q, -1, 1] = move("b", 0, q, dz=-1)
 
-    l_proj.wait()
-    where = pbuf.at[z, y, own_rows]
-    b_start_chain(0)
-    for hop in (1, -1, 2):
-        by[hop] = move("b", 0, 0, dy=hop)
-    x_swap = send(where, where, to_device(3 - x))
-    l_emb.wait()
-    mine = ebuf.at[pl.ds(pl.multiple_of(core * 128, 128), 128)]
-    e_copy = send(mine, mine, device(dc=1))
-    l_tgt.wait()
-    t_copy = send(target.at[:, other_rows], tbuf.at[my_docs], device(dx=2))
-
-    x_swap.wait_recv()
+    def b_y(hop):
+        by[hop].wait_recv()
+        b_own(2 if hop == 2 else -hop)
+
+    def b_step(step, q):
+        for sign in (1, -1):
+            if (q, sign, step) in bz:
+                bz[q, sign, step].wait_recv()
+                if step < 3 or (step == 3 and (sign == 1) == (q in (0, 2))):
+                    bz[q, sign, step + 1] = move("b", -sign * step, q, dz=sign)
 
     def a_y_sends(dz):
         ay[dz, 1] = move("a", dz, 0, dy=1)
@@ -134,35 +123,18 @@
             ay[dz, -1].wait_recv()
             ay[dz, 2] = move("a", dz, 1, dy=-1)
 
-    az[1, 1] = move("a", 0, 0, dz=1)
-    az[-1, 1] = move("a", 0, 0, dz=-1)
-    a_y_sends(0)
-    by[1].wait_recv()
-    b_start_chain(-1)
-    by[-1].wait_recv()
-    b_start_chain(1)
-    by[2].wait_recv()
-    b_start_chain(2)
-
-    def b_step(step, q):
-        for sign in (1, -1):
-            if (q, sign, step) in bz:
-                bz[q, sign, step].wait_recv()
-                if step < 3 or (step == 3 and (sign == 1) == (q in (0, 2))):
-                    bz[q, sign, step + 1] = move("b", -sign * step, q, dz=sign)
-
     def a_step(step):
         for sign in (1, -1):
             az[sign, step].wait_recv()
             if step < 3:
                 az[sign, step + 1] = move("a", -sign * step, 0, dz=sign)
             elif step == 3:
-                az[sign, 4] = move("a+" if sign == 1 else "a-", -sign * step, 0, dz=sign)
+                az[sign, 4] = move_half(0 if sign == 1 else 1, -sign * step, dz=sign)
+        a_y_sends(step)
         if step < 4:
-            a_y_sends(step)
             a_y_sends(-step)
-        else:
-            a_y_sends(4)
+
+    me8 = x * 2 + core
 
     def target_stats(block):
         rows = pl.ds(pl.multiple_of(block * 128, 128), 128)
@@ -175,36 +147,67 @@
         stats[me8, 0:1, rows] = jnp.sum(wp.T, axis=0, keepdims=True)
         stats[me8, 1:2, rows] = jnp.sum(lp.T, axis=0, keepdims=True)
 
-    me8 = x * 2 + core
-    stats[me8] = jnp.zeros((8, RING_DOCS), f32)
-
     def centroid_block(j):
         cols = pl.ds(pl.multiple_of(j * 128, 128), 128)
         c = cbuf[cols, :].astype(f32).T
         ct[:, cols] = c.astype(bf16)
         cn_ref[0:1, cols] = jnp.sum(c * c, axis=0, keepdims=True)
 
+    l_proj.wait()
+    where = pbuf.at[z, y, own_rows]
+    x_swap = send(where, where, to_device(3 - x))
+    az[1, 1] = move("a", 0, 0, dz=1)
+    az[-1, 1] = move("a", 0, 0, dz=-1)
+    a_y_sends(0)
+    l_emb.wait()
+    mine = ebuf.at[pl.ds(pl.multiple_of(core * 128, 128), 128)]
+    e_copy = send(mine, mine, device(dc=1))
+    stats[me8] = jnp.zeros((8, RING_DOCS), f32)
+
+    x_swap.wait_recv()
+    b_own(0)
+    for hop in (1, -1, 2):
+        by[hop] = move("b", 0, 0, dy=hop)
+    t_copy = send(target.at[:, other_rows], tbuf.at[my_docs], device(dx=2))
     l_cent.wait()
-    for step in (1, 2, 3, 4):
-        b_step(step, 0)
-        a_step(step)
-        for q in (-1, 1, 2):
-            b_step(step, q)
-        if step == 1:
-            a_y_forward(0)
-        else:
-            a_y_forward(step - 1)
-            a_y_forward(-(step - 1))
-        centroid_block(2 * step - 2)
-        centroid_block(2 * step - 1)
-        target_stats(xh * 4 + step - 1)
+    l_tgt.wait()
+    a_step(1)
+    a_y_forward(0)
+    a_step(2)
+    for hop in (1, -1, 2):
+        b_y(hop)
+    b_step(1, 0)
+    a_y_forward(1)
+    a_y_forward(-1)
+    centroid_block(0)
+    a_step(3)
+    for q in (-1, 1, 2):
+        b_step(1, q)
+    b_step(2, 0)
+    a_y_forward(2)
+    a_y_forward(-2)
+    centroid_block(1)
+    centroid_block(2)
+    a_step(4)
+    for q in (-1, 1, 2):
+        b_step(2, q)
+    b_step(3, 0)
+    a_y_forward(3)
+    a_y_forward(-3)
     a_y_forward(4)
-    t_copy.wait_recv()
-
-    @pl.loop(0, 4)
-    def _(i):
-        target_stats((1 - xh) * 4 + i)
-
+    centroid_block(3)
+    centroid_block(4)
+    target_stats(xh * 4)
+    for q in (-1, 1, 2):
+        b_step(3, q)
+    target_stats(xh * 4 + 1)
+    centroid_block(5)
+    centroid_block(6)
+    centroid_block(7)
+    target_stats(xh * 4 + 2)
+    target_stats(xh * 4 + 3)
+    for q in (0, -1, 1, 2):
+        b_step(4, q)
     e_copy.wait_recv()
     for dz in (0, 1, -1, 2, -2, 3, -3, 4):
         ay[dz, -1 if dz % 2 == 0 else 1].wait_recv()
@@ -252,6 +255,12 @@
         ft[0:HALF, rows] = feat[0, rows, :].astype(f32).T.astype(bf16)
         ft[HALF:DZ, rows] = feat[1, rows, :].astype(f32).T.astype(bf16)
 
+    t_copy.wait_recv()
+
+    @pl.loop(0, 4)
+    def _(i):
+        target_stats((1 - xh) * 4 + i)
+
     inner(0)
     transpose_features(0)
     for dx in (1, 3, 2):
@@ -355,30 +364,36 @@
 
     push_pair(0)
     push_pair(2)
+    pulls[2] = pull_block(2)
+    combine(0)
+    combine(1)
     push_pair(4)
+    pulls[1] = pull_block(1)
+    pull_sum(2)
+    combine(2)
+    combine(3)
     push_pair(6)
-    combine(0)
-    pulls[2] = pull_block(2)
-    combine(1)
-    pulls[1] = pull_block(1)
-    combine(2)
-    pull_sum(2)
     pulls[3] = pull_block(3)
-    combine(3)
     pull_sum(1)
+    y_total(0)
+    y_total(1)
     pulls[0] = pull_block(0)
     pull_sum(3)
     combine(4)
-    pull_sum(0)
+    combine(5)
     for copy in lsy:
         copy.wait_recv()
     lz[z] = (ly[0] + ly[1]) + (ly[2] + ly[3])
     lsz = [send(lz.at[z], lz.at[z], device(dz=d)) for d in range(1, NZ)]
-    combine(5)
+    y_total(2)
+    y_total(3)
+    pull_sum(0)
     combine(6)
     combine(7)
-    for i in range(8):
-        y_total(i)
+    y_total(4)
+    y_total(5)
+    y_total(6)
+    y_total(7)
     for dx in (1, 3, 2):
         gs[dx].wait_recv()
     gp_ref[...] = pown[...] + gx[0].astype(f32) + gx[1].astype(f32) + gx[2].astype(f32)
@@ -405,9 +420,15 @@
         copy.wait_send()
 
 
+def hand_over(gp, gc, loss, gp_out, gc_out, loss_out):
+    gp_out[...] = gp[...]
+    gc_out[...] = gc[...]
+    loss_out[0, 0] = loss[0, 0]
+
+
 def per_device(embeddings, projection, centroids, target):
     vmem = pltpu.VMEM
-    gp, gct, loss = pl.pallas_call(
+    outs = pl.pallas_call(
         body,
         name="cluster_head",
         out_shape=(
@@ -458,7 +479,18 @@
         ),
         cost_estimate=pl.CostEstimate(flops=7_500_000_000, bytes_accessed=9_000_000, transcendentals=3_000_000),
     )(embeddings, projection, centroids, target)
-    return gp, gct.T, loss[0, 0]
+    gp, gct, loss = pl.pallas_call(
+        hand_over,
+        name="hand_over",
+        out_shape=(
+            jax.ShapeDtypeStruct((DOCS_DEV, DZ), f32),
+            jax.ShapeDtypeStruct((16, 2 * CENTS), f32),
+            jax.ShapeDtypeStruct((1, 1), f32),
+        ),
+        in_specs=[pl.BlockSpec(memory_space=vmem)] * 3,
+        out_specs=(pl.BlockSpec(memory_space=vmem),) * 2 + (pl.BlockSpec(memory_space=pltpu.SMEM),),
+    )(*outs)
+    return gp, gct.T, loss.reshape(())
 
 
 def solution(mesh):

time: 132 us -> 101 us (0.77); the launches traced: 130 us -> 101 us
  Pallas kernels: 125 us -> 99.9 us
  local copies, waits for them, and re-layouts: 4.65 us -> 0 us
    pallas_call x1, Pallas kernels: 125 us -> 97.9 us  [per_device(): pl.pallas_call(body, name='cluster_head', out_shape=(jax.ShapeDtypeStruct...]
    unnamed x2 -> x0, local copies, waits for them, and re-layouts: 3.45 us -> none
    pallas_call x0 -> x1, Pallas kernels: none -> 2 us  [per_device(): pl.pallas_call(hand_over, name='hand_over', out_shape=(jax.ShapeDtypeStru...]
where the time goes in v2:
time: 101 us
  Pallas kernels  99.9 us (99%)
    pallas_call x1, Pallas kernels, per_device(): pl.pallas_call(body, name='cluster_head', out_shape=(jax.ShapeDtypeStruct...  97.9 us

profile of v2, /device:TPU:8, one launch (start us, length us, event | category | flops | bytes accessed | tf_op | source)
XLA Modules:
  0.0 100.7 jit_solution(2541064592456870577)
XLA Ops:
  0.6 97.9 %cluster_head.1 = (f32[128,1024]{1,0:T(8,128)}, f32[16,2048]{1,0:T(8,128)}, f32[8,128]{1,0:T(8,128)}) custom-call(bf16[128,4096]{1,0:T(8,128)(2,1)} %emb.1, bf16[64,1024]{1,0:T(8,128)(2,1)} %proj.1, bf16[2048,1024]{1,0:T(8,128)(2,1)} %cent.1, bf16[512,2048]{1,0:T(8,128)(2,1)} %target.1), custom_call_target="tpu_custom_call" | custom-call | flops 7500000256 | bytes 9000000 | tf_op jit(solution)/shard_map/cluster_head/pallas_call | solution.py:431
  98.5 2.0 %hand_over.1 = (f32[128,1024]{1,0:T(8,128)}, f32[16,2048]{1,0:T(8,128)}, f32[1,1]{1,0:T(1,128)}) custom-call(f32[128,1024]{1,0:T(8,128)} %get-tuple-element.9.gp, f32[16,2048]{1,0:T(8,128)} %get-tuple-element.10.gc, f32[8,128]{1,0:T(8,128)} %get-tuple-element.11.loss), custom_call_target="tpu_custom_call" | custom-call | tf_op jit(solution)/shard_map/hand_over/pallas_call | solution.py:482

commit v3 on v2

v3 whole, which is shorter than its diff:
```python
import jax
import jax.numpy as jnp
from jax import lax
from jax.experimental import pallas as pl
from jax.experimental.pallas import tpu as pltpu
from jax.sharding import PartitionSpec as P

NZ, NY, NX = 8, 4, 4
DIN, DZ, HALF, QUARTER = 4096, 1024, 512, 256
DOCS_DEV, CHIP_DOCS, RING_DOCS = 128, 256, 1024
CENTS = 1024
DOCS = 32768
SCALE = 64.0
Y_FIRST, Z_FIRST = 896, 128
ORDER = (4, 3, -3, 2, -2, 1, -1, 0)
N_SEM = 288
bf16, f32 = jnp.bfloat16, jnp.float32


def body(
    emb, proj, cent, target,
    gp_ref, gc_ref, loss_ref,
    pbuf, ebuf, cbuf, ct, tbuf, feat, ft, kbuf, cbf, early, late, ab, rowg_ref, cn_ref, colg_ref,
    rs, rfwd, rone, rcomb, csend, zsend, zrecv, zb, zbr, ybs, ybr, ysum, xsend, xrecv,
    psend, pown, precv, gsend, gx, ly, lz,
    send_sems, recv_sems, local_sems,
):
    wide, narrow = lax.axis_index("wide"), lax.axis_index("narrow")
    z, y, xh = wide // 8, (wide // 2) % 4, wide % 2
    xl, core = narrow // 2, narrow % 2
    x = xh * 2 + xl

    def device(dx=0, dy=0, dz=0, dc=0):
        tx, ty, tz, tc = (x + dx + NX) % NX, (y + dy + NY) % NY, (z + dz + NZ) % NZ, (core + dc) % 2
        return (tz * 8 + ty * 2 + tx // 2, (tx % 2) * 2 + tc)

    def to_device(tx):
        return (z * 8 + y * 2 + tx // 2, (tx % 2) * 2 + core)

    def zi(dz):
        return (z + dz + NZ) % NZ

    def yi(dy):
        return (y + dy + NY) % NY

    def xi(dx):
        return (x + dx + NX) % NX

    copies = []

    def send(src, dst, target_device):
        number = len(copies)
        copy = pltpu.make_async_remote_copy(
            src_ref=src, dst_ref=dst, send_sem=send_sems.at[number], recv_sem=recv_sems.at[number],
            device_id=target_device, device_id_type=pl.DeviceIdType.MESH,
        )
        copy.start()
        copies.append(copy)
        return copy

    locals_ = []

    def local(src, dst):
        copy = pltpu.make_async_copy(src, dst, local_sems.at[len(locals_)])
        copy.start()
        locals_.append(copy)
        return copy

    own_rows = pl.ds(pl.multiple_of(xh * 64, 64), 64)
    l_proj = []
    for r in range(2):
        cols = pl.ds(pl.multiple_of(core * HALF + r * QUARTER, QUARTER), QUARTER)
        l_proj.append(local(proj.at[:, cols], pbuf.at[r, z, y, own_rows]))
    l_emb = local(emb, ebuf.at[pl.ds(pl.multiple_of(core * 128, 128), 128)])
    j_rows = pl.ds(pl.multiple_of(xh * CENTS, CENTS), CENTS)
    other_rows = pl.ds(pl.multiple_of((1 - xh) * CENTS, CENTS), CENTS)
    my_docs = pl.ds(pl.multiple_of(xh * 512, 512), 512)
    l_cent = local(cent.at[j_rows], cbuf)
    l_tgt = local(target.at[:, j_rows], tbuf.at[my_docs])

    ring = [(dx, dc) for dx in range(NX) for dc in range(2) if (dx, dc) != (0, 0)]
    peers = [device(dx=dx, dc=dc) for dx, dc in ring]
    peers += [device(dz=d) for d in range(1, NZ)] + [device(dy=d) for d in range(1, NY)]
    barrier = pltpu.get_barrier_semaphore()
    for peer in peers:
        pl.semaphore_signal(barrier, inc=1, device_id=peer, device_id_type=pl.DeviceIdType.MESH)
    pl.semaphore_wait(barrier, len(peers))

    other_half = pl.ds(pl.multiple_of((1 - xh) * 64, 64), 64)

    class Gather:
        def __init__(self, r):
            self.buf = pbuf.at[r]
            self.bz, self.az, self.ay, self.by = {}, {}, {}, {}

        def move(self, part, at_z, at_y, **hop):
            where = self.buf.at[zi(at_z), yi(at_y), own_rows if part == "a" else other_half]
            return send(where, where, device(**hop))

        def move_half(self, half, at_z, **hop):
            start = pl.multiple_of(xh * 64 + half * 32, 32)
            where = self.buf.at[zi(at_z), y, pl.ds(start, 32)]
            return send(where, where, device(**hop))

        def b_own(self, q):
            for sign in (1, -1):
                self.bz[q, sign, 1] = self.move("b", 0, q, dz=sign)

        def b_y(self, hop):
            self.by[hop].wait_recv()
            self.b_own(2 if hop == 2 else -hop)

        def b_step(self, step, q):
            for sign in (1, -1):
                if (q, sign, step) in self.bz:
                    self.bz[q, sign, step].wait_recv()
                    if step < 3 or (step == 3 and (sign == 1) == (q in (0, 2))):
                        self.bz[q, sign, step + 1] = self.move("b", -sign * step, q, dz=sign)

        def a_y_sends(self, dz):
            for sign in (1, -1):
                self.ay[dz, sign] = self.move("a", dz, 0, dy=sign)

        def a_y_forward(self, dz):
            sign = 1 if dz % 2 == 0 else -1
            self.ay[dz, sign].wait_recv()
            self.ay[dz, 2] = self.move("a", dz, -sign, dy=sign)

        def a_step(self, step):
            for sign in (1, -1):
                self.az[sign, step].wait_recv()
                if step < 3:
                    self.az[sign, step + 1] = self.move("a", -sign * step, 0, dz=sign)
                elif step == 3:
                    self.az[sign, 4] = self.move_half(0 if sign == 1 else 1, -sign * step, dz=sign)
            self.a_y_sends(step)
            if step < 4:
                self.a_y_sends(-step)

        def group(self, g):
            if g == 0:
                where = self.buf.at[z, y, own_rows]
                self.x_swap = send(where, where, to_device(3 - x))
                for sign in (1, -1):
                    self.az[sign, 1] = self.move("a", 0, 0, dz=sign)
                self.a_y_sends(0)
            elif g == 1:
                self.x_swap.wait_recv()
                self.b_own(0)
                for hop in (1, -1, 2):
                    self.by[hop] = self.move("b", 0, 0, dy=hop)
            elif g in (2, 4, 7, 10):
                self.a_step({2: 1, 4: 2, 7: 3, 10: 4}[g])
            elif g == 3:
                self.a_y_forward(0)
            elif g == 5:
                for hop in (1, -1, 2):
                    self.b_y(hop)
                self.b_step(1, 0)
            elif g in (6, 9, 12):
                step = g // 3 - 1
                self.a_y_forward(step)
                self.a_y_forward(-step)
                if step == 3:
                    self.a_y_forward(4)
            elif g in (8, 11, 13):
                step = {8: 1, 11: 2, 13: 3}[g]
                for q in (-1, 1, 2):
                    self.b_step(step, q)
                if step < 3:
                    self.b_step(step + 1, 0)
            else:
                for q in (0, -1, 1, 2):
                    self.b_step(4, q)
                for dz in (0, 1, -1, 2, -2, 3, -3, 4):
                    self.ay[dz, -1 if dz % 2 == 0 else 1].wait_recv()
                    self.ay[dz, 2].wait_recv()

    me8 = x * 2 + core

    def put_stat(stat, block, partial):
        cols = pl.ds(pl.multiple_of((block % 4) * 128, 128), 128)
        early[me8, block // 4, stat:stat + 1, cols] = jnp.sum(partial.T, axis=0, keepdims=True)

    def target_stats(block):
        rows = pl.ds(pl.multiple_of(block * 128, 128), 128)
        wp = jnp.zeros((128, 128), f32)
        lp = jnp.zeros((128, 128), f32)
        for lane in range(8):
            t = tbuf[rows, lane * 128:(lane + 1) * 128].astype(f32)
            wp = wp + t
            lp = lp + t * jnp.log(t)
        put_stat(0, block, wp)
        put_stat(1, block, lp)

    def centroid_block(j):
        cols = pl.ds(pl.multiple_of(j * 128, 128), 128)
        c = cbuf[cols, :].astype(f32).T
        ct[:, cols] = c.astype(bf16)
        cn_ref[0:1, cols] = jnp.sum(c * c, axis=0, keepdims=True)

    rounds = [Gather(0), Gather(1)]
    fx, fc = {}, {}

    def chip_rows(dx):
        return pl.ds(pl.multiple_of(xi(dx) * CHIP_DOCS, CHIP_DOCS), CHIP_DOCS)

    def feat_send(r, at_x, **hop):
        where = feat.at[2 * core + r, chip_rows(at_x)]
        return send(where, where, device(**hop))

    def finish_round(r):
        rounds[r].group(14)
        if r == 0:
            e_copy.wait_recv()
        own = jnp.dot(ebuf[...], pbuf[r].reshape(DIN, QUARTER), preferred_element_type=f32)
        feat[2 * core + r, chip_rows(0), :] = own.astype(bf16)
        fx[r, 1] = feat_send(r, 0, dx=1)
        fx[r, 3] = feat_send(r, 0, dx=-1)
        fc[r, 0] = feat_send(r, 0, dc=1)
        fx[r, 2] = feat_send(r, 0, dx=2)

    l_proj[0].wait()
    rounds[0].group(0)
    l_emb.wait()
    mine = ebuf.at[pl.ds(pl.multiple_of(core * 128, 128), 128)]
    e_copy = send(mine, mine, device(dc=1))
    early[me8] = jnp.zeros((2, 4, 512), f32)
    late[me8] = jnp.zeros((8, 128), f32)
    l_proj[1].wait()
    rounds[1].group(0)
    rounds[0].group(1)
    rounds[1].group(1)
    t_copy = send(target.at[:, other_rows], tbuf.at[my_docs], device(dx=2))
    l_cent.wait()
    l_tgt.wait()
    rounds[0].group(2)
    rounds[0].group(3)
    rounds[0].group(4)
    rounds[0].group(5)
    rounds[0].group(6)
    rounds[1].group(2)
    centroid_block(0)
    rounds[0].group(7)
    rounds[1].group(3)
    rounds[0].group(8)
    centroid_block(1)
    rounds[1].group(4)
    rounds[0].group(9)
    rounds[1].group(5)
    centroid_block(2)
    rounds[0].group(10)
    rounds[1].group(6)
    rounds[0].group(11)
    centroid_block(3)
    rounds[1].group(7)
    rounds[0].group(12)
    rounds[1].group(8)
    centroid_block(4)
    rounds[0].group(13)
    rounds[1].group(9)
    rounds[1].group(10)
    centroid_block(5)
    rounds[1].group(11)
    rounds[1].group(12)
    finish_round(0)
    rounds[1].group(13)
    centroid_block(6)
    centroid_block(7)
    target_stats(xh * 4 + 0)
    target_stats(xh * 4 + 1)
    target_stats(xh * 4 + 2)
    target_stats(xh * 4 + 3)
    finish_round(1)

    def inner(dx):
        fc[0, dx].wait_recv()
        fc[1, dx].wait_recv()
        rows = chip_rows(dx)
        parts = [feat[i, rows, :] for i in range(4)]
        f = jnp.concatenate(parts, axis=1)
        g = jnp.dot(f, ct[...], preferred_element_type=f32)
        sq = jnp.zeros((CHIP_DOCS, QUARTER), f32)
        for part in parts:
            sq = sq + part.astype(f32) * part.astype(f32)
        zn = 1.0 + jnp.sum(sq, axis=1, keepdims=True)
        kp = jnp.zeros((CHIP_DOCS, 128), f32)
        cp = jnp.zeros((CHIP_DOCS, 128), f32)
        for lane in range(8):
            cols = slice(lane * 128, (lane + 1) * 128)
            u = (zn + cn_ref[0:1, cols]) - 2.0 * g[:, cols]
            r = pl.reciprocal(u, approx=True)
            k = r * (2.0 - u * r)
            kbuf[rows, cols] = k
            kp = kp + k
            cp = cp + tbuf[rows, cols].astype(f32) * jnp.log(u)
        for h in range(2):
            half = slice(h * 128, (h + 1) * 128)
            if dx == 2:
                late[me8, h:h + 1, :] = jnp.sum(kp[half].T, axis=0, keepdims=True)
                late[me8, 2 + h:3 + h, :] = jnp.sum(cp[half].T, axis=0, keepdims=True)
            else:
                put_stat(2, xi(dx) * 2 + h, kp[half])
                put_stat(3, xi(dx) * 2 + h, cp[half])

    def transpose_features(dx):
        rows = chip_rows(dx)
        for i in range(4):
            ft[i * QUARTER:(i + 1) * QUARTER, rows] = feat[i, rows, :].astype(f32).T.astype(bf16)

    t_copy.wait_recv()

    @pl.loop(0, 4)
    def _(i):
        target_stats((1 - xh) * 4 + i)

    def pass_on(r, dx):
        fx[r, dx].wait_recv()
        fc[r, NX - dx] = feat_send(r, NX - dx, dc=1)

    for dx in (1, 3, 2):
        pass_on(0, dx)
    inner(0)
    transpose_features(0)
    pass_on(1, 1)
    pass_on(1, 3)
    inner(1)
    pass_on(1, 2)
    inner(3)
    st = [send(early.at[me8], early.at[me8], device(dx=dx, dc=dc)) for dx, dc in ring]
    inner(2)
    st += [send(late.at[me8], late.at[me8], device(dx=dx, dc=dc)) for dx, dc in ring]
    for dx in (1, 3, 2):
        transpose_features(dx)
    for copy in st:
        copy.wait_recv()

    def lanes(parts):
        return jnp.concatenate(parts, axis=1)

    def totals(stat):
        tot = jnp.zeros((1, RING_DOCS), f32)
        for i in range(8):
            tot = tot + lanes([early[i, 0, stat:stat + 1, :], early[i, 1, stat:stat + 1, :]])
        if stat < 2:
            return tot
        for c in range(2):
            tot = tot + lanes([
                late[2 * ((b // 2 + 2) % 4) + c, (stat - 2) * 2 + b % 2:(stat - 2) * 2 + b % 2 + 1, :]
                for b in range(8)
            ])
        return tot

    wsum, ksum = totals(0), totals(2)
    ra, rb = SCALE / wsum, SCALE / ksum
    for block in range(8):
        rows = slice(block * 128, (block + 1) * 128)
        ab[0, rows, :] = jnp.broadcast_to(ra[:, rows], (128, 128)).T
        ab[1, rows, :] = jnp.broadcast_to(rb[:, rows], (128, 128)).T

    colg_ref[...] = jnp.zeros((8, CENTS), f32)

    @pl.loop(0, 8)
    def _(block):
        rows = pl.ds(pl.multiple_of(block * 128, 128), 128)
        a, b = ab[0, rows, :], ab[1, rows, :]
        rp = jnp.zeros((128, 128), f32)
        for lane in range(8):
            cols = slice(lane * 128, (lane + 1) * 128)
            k = kbuf[rows, cols]
            cf = (k * (tbuf[rows, cols].astype(f32) * a - k * b)).astype(bf16)
            cbf[rows, cols] = cf
            cf = cf.astype(f32)
            rp = rp + cf
            colg_ref[:, cols] += jnp.sum(cf.reshape(16, 8, 128), axis=0)
        rowg_ref[rows, :] = jnp.broadcast_to(jnp.sum(rp, axis=1, keepdims=True), (128, 128))

    colg = jnp.sum(colg_ref[...], axis=0, keepdims=True)
    fwd, one, comb, zs, zfirst, yb = {}, {}, {}, {}, {}, {}

    def push_pair(first):
        rows = [pl.ds(pl.multiple_of(zi(ORDER[i]) * 128, 128), 128) for i in (first, first + 1)]
        lhs = jnp.concatenate([ft[r, :] for r in rows], axis=0)
        prod = jnp.dot(lhs, cbf[...], preferred_element_type=f32)
        for k, i in enumerate((first, first + 1)):
            part = prod[k * 128:(k + 1) * 128]
            part = -2.0 * (part - colg * ct[rows[k], :].astype(f32))
            part = part.astype(bf16)
            rs[i] = part[:, :Y_FIRST].reshape(4, 32, Y_FIRST)
            zb[i] = part[:, Y_FIRST:]
            sign = 1 if i % 2 == 0 else -1
            fwd[i] = send(rs.at[i, yi(2)], rfwd.at[i], device(dy=sign))
            one[i] = send(rs.at[i, yi(-sign)], rone.at[i], device(dy=-sign))
            if ORDER[i] != 0:
                zfirst[i] = send(zb.at[i], zbr.at[i], device(dz=ORDER[i]))

    def combine(i):
        sign = 1 if i % 2 == 0 else -1
        fwd[i].wait_recv()
        csend[i] = (rs[i, yi(sign)].astype(f32) + rfwd[i].astype(f32)).astype(bf16)
        comb[i] = send(csend.at[i], rcomb.at[i], device(dy=sign))

    def y_total(i):
        one[i].wait_recv()
        comb[i].wait_recv()
        total = rs[i, y].astype(f32) + rone[i].astype(f32) + rcomb[i].astype(f32)
        if ORDER[i] == 0:
            ysum[:, :Y_FIRST] = total
        else:
            zsend[i] = total.astype(bf16)
            zs[i] = send(zsend.at[i], zrecv.at[i], device(dz=ORDER[i]))

    def z_first_total():
        total = zb[7].astype(f32)
        for i in range(7):
            zfirst[i].wait_recv()
            total = total + zbr[i].astype(f32)
        ybs[...] = total.astype(bf16).reshape(4, 32, Z_FIRST)
        for d in range(1, NY):
            yb[d] = send(ybs.at[yi(d)], ybr.at[d - 1], device(dy=d))

    def pull_block(dx):
        rows = chip_rows(dx)
        pull = jnp.dot(cbf[rows, :], cbuf[...], preferred_element_type=f32)
        rg = rowg_ref[rows, :]
        blocks = []
        for h in range(4):
            f = feat[h, rows, :].astype(f32)
            rgw = jnp.concatenate([rg] * 2, axis=1)
            blocks.append(2.0 * (rgw * f - pull[:, h * QUARTER:(h + 1) * QUARTER]))
        part = jnp.concatenate(blocks, axis=1)
        psend[dx % NX, 0] = part[0:128].astype(bf16)
        psend[dx % NX, 1] = part[128:256].astype(bf16)
        return send(psend.at[dx % NX, 1 - core], precv.at[dx % NX], device(dc=1))

    pulls, gs = {}, {}

    def pull_sum(dx):
        pulls[dx].wait_recv()
        both = psend[dx, core].astype(f32) + precv[dx].astype(f32)
        if dx == 0:
            pown[...] = both
        else:
            gsend[dx - 1] = both.astype(bf16)
            gs[dx] = send(gsend.at[dx - 1], gx.at[dx - 1], device(dx=dx))

    push_pair(0)
    push_pair(2)
    tlog, clog = totals(1), totals(3)
    row_loss = (tlog + clog) / wsum - jnp.log(wsum) + jnp.log(ksum)
    ly[y] = jnp.broadcast_to(jnp.sum(row_loss, axis=1, keepdims=True), (8, 128))
    lsy = [send(ly.at[y], ly.at[y], device(dy=d)) for d in range(1, NY)]
    pulls[2] = pull_block(2)
    combine(0)
    combine(1)
    push_pair(4)
    pulls[1] = pull_block(1)
    pull_sum(2)
    combine(2)
    combine(3)
    push_pair(6)
    pulls[3] = pull_block(3)
    pull_sum(1)
    z_first_total()
    y_total(0)
    y_total(1)
    pulls[0] = pull_block(0)
    pull_sum(3)
    combine(4)
    combine(5)
    for copy in lsy:
        copy.wait_recv()
    lz[z] = (ly[0] + ly[1]) + (ly[2] + ly[3])
    lsz = [send(lz.at[z], lz.at[z], device(dz=d)) for d in range(1, NZ)]
    y_total(2)
    y_total(3)
    pull_sum(0)
    combine(6)
    combine(7)
    y_total(4)
    y_total(5)
    y_total(6)
    y_total(7)
    for dx in (1, 3, 2):
        gs[dx].wait_recv()
    gp_ref[...] = pown[...] + gx[0].astype(f32) + gx[1].astype(f32) + gx[2].astype(f32)
    for copy in lsz:
        copy.wait_recv()
    total = lz[0]
    for i in range(1, NZ):
        total = total + lz[i]
    loss_ref[...] = total * (1.0 / DOCS)
    for d in range(1, NY):
        yb[d].wait_recv()
    for i in range(7):
        zs[i].wait_recv()
    for h in range(2):
        rows = slice(h * 16, (h + 1) * 16)
        part = ysum[rows, :Y_FIRST]
        for i in range(7):
            part = part + zrecv[i, rows, :].astype(f32)
        ysum[rows, :Y_FIRST] = part
        part = ybs[y, rows, :].astype(f32)
        for i in range(3):
            part = part + ybr[i, rows, :].astype(f32)
        ysum[rows, Y_FIRST:] = part
    xsend[...] = ysum[pl.ds(pl.multiple_of((1 - xh) * 16, 16), 16), :].astype(bf16)
    last = send(xsend, xrecv, device(dx=2))
    gc_ref[:, j_rows] = ysum[pl.ds(pl.multiple_of(xh * 16, 16), 16), :]
    last.wait_recv()
    gc_ref[:, other_rows] = xrecv[...].astype(f32)
    for copy in copies:
        copy.wait_send()


def hand_over(gp, gc, loss, gp_out, gc_out, loss_out):
    gp_out[...] = gp[...]
    gc_out[...] = gc[...]
    loss_out[0, 0] = loss[0, 0]


def per_device(embeddings, projection, centroids, target):
    vmem = pltpu.VMEM
    outs = pl.pallas_call(
        body,
        name="cluster_head",
        out_shape=(
            jax.ShapeDtypeStruct((DOCS_DEV, DZ), f32),
            jax.ShapeDtypeStruct((16, 2 * CENTS), f32),
            jax.ShapeDtypeStruct((8, 128), f32),
        ),
        in_specs=[pl.BlockSpec(memory_space=pl.ANY)] * 4,
        out_specs=(pl.BlockSpec(memory_space=vmem),) * 3,
        scratch_shapes=[
            vmem((2, NZ, NY, 128, QUARTER), bf16),
            vmem((CHIP_DOCS, DIN), bf16),
            vmem((CENTS, DZ), bf16),
            vmem((DZ, CENTS), bf16),
            vmem((RING_DOCS, CENTS), bf16),
            vmem((4, RING_DOCS, QUARTER), bf16),
            vmem((DZ, RING_DOCS), bf16),
            vmem((RING_DOCS, CENTS), f32),
            vmem((RING_DOCS, CENTS), bf16),
            vmem((8, 2, 4, 512), f32),
            vmem((8, 8, 128), f32),
            vmem((2, RING_DOCS, 128), f32),
            vmem((RING_DOCS, 128), f32),
            vmem((8, CENTS), f32),
            vmem((8, CENTS), f32),
            vmem((8, 4, 32, Y_FIRST), bf16),
            vmem((8, 32, Y_FIRST), bf16),
            vmem((8, 32, Y_FIRST), bf16),
            vmem((8, 32, Y_FIRST), bf16),
            vmem((8, 32, Y_FIRST), bf16),
            vmem((7, 32, Y_FIRST), bf16),
            vmem((7, 32, Y_FIRST), bf16),
            vmem((8, 128, Z_FIRST), bf16),
            vmem((7, 128, Z_FIRST), bf16),
            vmem((4, 32, Z_FIRST), bf16),
            vmem((3, 32, Z_FIRST), bf16),
            vmem((32, CENTS), f32),
            vmem((16, CENTS), bf16),
            vmem((16, CENTS), bf16),
            vmem((4, 2, 128, DZ), bf16),
            vmem((128, DZ), f32),
            vmem((4, 128, DZ), bf16),
            vmem((3, 128, DZ), bf16),
            vmem((3, 128, DZ), bf16),
            vmem((NY, 8, 128), f32),
            vmem((NZ, 8, 128), f32),
            pltpu.SemaphoreType.DMA((N_SEM,)),
            pltpu.SemaphoreType.DMA((N_SEM,)),
            pltpu.SemaphoreType.DMA((5,)),
        ],
        compiler_params=pltpu.CompilerParams(
            collective_id=0, has_side_effects=True, vmem_limit_bytes=60 * 2**20
        ),
        cost_estimate=pl.CostEstimate(flops=7_500_000_000, bytes_accessed=9_000_000, transcendentals=3_000_000),
    )(embeddings, projection, centroids, target)
    gp, gct, loss = pl.pallas_call(
        hand_over,
        name="hand_over",
        out_shape=(
            jax.ShapeDtypeStruct((DOCS_DEV, DZ), f32),
            jax.ShapeDtypeStruct((16, 2 * CENTS), f32),
            jax.ShapeDtypeStruct((1, 1), f32),
        ),
        in_specs=[pl.BlockSpec(memory_space=vmem)] * 3,
        out_specs=(pl.BlockSpec(memory_space=vmem),) * 2 + (pl.BlockSpec(memory_space=pltpu.SMEM),),
    )(*outs)
    return gp, gct.T, loss.reshape(())


def solution(mesh):
    placed = (P(("wide", "narrow"), None), P("wide", None), P("narrow", None), P("wide", "narrow"))
    return jax.shard_map(
        per_device,
        mesh=mesh,
        in_specs=placed,
        out_specs=(P(("wide", "narrow"), None), P("narrow", "wide"), P()),
        check_vma=False,
    )
```

time: 101 us -> 95.7 us (0.948)
  Pallas kernels: 99.9 us -> 94.8 us
    pallas_call x1, Pallas kernels: 97.9 us -> 92.8 us  [per_device(): pl.pallas_call(body, name='cluster_head', out_shape=(jax.ShapeDtypeStruct...]
where the time goes in v3:
time: 95.7 us; the launch traced here: 95.6 us
  Pallas kernels  94.8 us (99%)
    pallas_call x1, Pallas kernels, per_device(): pl.pallas_call(body, name='cluster_head', out_shape=(jax.ShapeDtypeStruct...  92.8 us
    pallas_call x1, Pallas kernels, per_device(): pl.pallas_call(hand_over, name='hand_over', out_shape=(jax.ShapeDtypeStru...  2 us

profile of v3, /device:TPU:8, one launch (start us, length us, event | category | flops | bytes accessed | tf_op | source)
XLA Modules:
  0.0 95.6 jit_solution(15886593786615644850)
XLA Ops:
  0.6 92.8 %cluster_head.1 = (f32[128,1024]{1,0:T(8,128)}, f32[16,2048]{1,0:T(8,128)}, f32[8,128]{1,0:T(8,128)}) custom-call(bf16[128,4096]{1,0:T(8,128)(2,1)} %emb.1, bf16[64,1024]{1,0:T(8,128)(2,1)} %proj.1, bf16[2048,1024]{1,0:T(8,128)(2,1)} %cent.1, bf16[512,2048]{1,0:T(8,128)(2,1)} %target.1), custom_call_target="tpu_custom_call" | custom-call | flops 7500000256 | bytes 9000000 | tf_op jit(solution)/shard_map/cluster_head/pallas_call | solution.py:524
  93.4 2.0 %hand_over.1 = (f32[128,1024]{1,0:T(8,128)}, f32[16,2048]{1,0:T(8,128)}, f32[1,1]{1,0:T(1,128)}) custom-call(f32[128,1024]{1,0:T(8,128)} %get-tuple-element.9.gp, f32[16,2048]{1,0:T(8,128)} %get-tuple-element.10.gc, f32[8,128]{1,0:T(8,128)} %get-tuple-element.11.loss), custom_call_target="tpu_custom_call" | custom-call | tf_op jit(solution)/shard_map/hand_over/pallas_call | solution.py:580

commit v4 on v3

--- a/solution.py
+++ b/solution.py
@@ -271,6 +271,7 @@
     target_stats(xh * 4 + 1)
     target_stats(xh * 4 + 2)
     target_stats(xh * 4 + 3)
+    gathered = len(copies)
     finish_round(1)
 
     def inner(dx):
@@ -322,6 +323,8 @@
         pass_on(0, dx)
     inner(0)
     transpose_features(0)
+    for copy in copies[:gathered]:
+        copy.wait_send()
     pass_on(1, 1)
     pass_on(1, 3)
     inner(1)
@@ -494,22 +497,21 @@
         yb[d].wait_recv()
     for i in range(7):
         zs[i].wait_recv()
-    for h in range(2):
-        rows = slice(h * 16, (h + 1) * 16)
-        part = ysum[rows, :Y_FIRST]
+    def final(h):
+        rows = pl.ds(pl.multiple_of(h * 16, 16), 16)
+        a, b = ysum[rows, :Y_FIRST], ybs[y, rows, :].astype(f32)
         for i in range(7):
-            part = part + zrecv[i, rows, :].astype(f32)
-        ysum[rows, :Y_FIRST] = part
-        part = ybs[y, rows, :].astype(f32)
+            a = a + zrecv[i, rows, :].astype(f32)
         for i in range(3):
-            part = part + ybr[i, rows, :].astype(f32)
-        ysum[rows, Y_FIRST:] = part
-    xsend[...] = ysum[pl.ds(pl.multiple_of((1 - xh) * 16, 16), 16), :].astype(bf16)
+            b = b + ybr[i, rows, :].astype(f32)
+        return jnp.concatenate([a, b], axis=1)
+
+    xsend[...] = final(1 - xh).astype(bf16)
     last = send(xsend, xrecv, device(dx=2))
-    gc_ref[:, j_rows] = ysum[pl.ds(pl.multiple_of(xh * 16, 16), 16), :]
+    gc_ref[:, j_rows] = final(xh)
     last.wait_recv()
     gc_ref[:, other_rows] = xrecv[...].astype(f32)
-    for copy in copies:
+    for copy in copies[gathered:]:
         copy.wait_send()
 
 

time: 95.7 us -> 95.4 us (level)
  no operation moved by 1% of the time
where the time goes in v4:
time: 95.4 us; the launch traced here: 95.3 us
  Pallas kernels  94.5 us (99%)
    pallas_call x1, Pallas kernels, per_device(): pl.pallas_call(body, name='cluster_head', out_shape=(jax.ShapeDtypeStruct...  92.5 us
    pallas_call x1, Pallas kernels, per_device(): pl.pallas_call(hand_over, name='hand_over', out_shape=(jax.ShapeDtypeStru...  2 us

profile of v4, /device:TPU:8, one launch (start us, length us, event | category | flops | bytes accessed | tf_op | source)
XLA Modules:
  0.0 95.3 jit_solution(10837488159712974821)
XLA Ops:
  0.6 92.5 %cluster_head.1 = (f32[128,1024]{1,0:T(8,128)}, f32[16,2048]{1,0:T(8,128)}, f32[8,128]{1,0:T(8,128)}) custom-call(bf16[128,4096]{1,0:T(8,128)(2,1)} %emb.1, bf16[64,1024]{1,0:T(8,128)(2,1)} %proj.1, bf16[2048,1024]{1,0:T(8,128)(2,1)} %cent.1, bf16[512,2048]{1,0:T(8,128)(2,1)} %target.1), custom_call_target="tpu_custom_call" | custom-call | flops 7500000256 | bytes 9000000 | tf_op jit(solution)/shard_map/cluster_head/pallas_call | solution.py:526
  93.2 2.0 %hand_over.1 = (f32[128,1024]{1,0:T(8,128)}, f32[16,2048]{1,0:T(8,128)}, f32[1,1]{1,0:T(1,128)}) custom-call(f32[128,1024]{1,0:T(8,128)} %get-tuple-element.9.gp, f32[16,2048]{1,0:T(8,128)} %get-tuple-element.10.gc, f32[8,128]{1,0:T(8,128)} %get-tuple-element.11.loss), custom_call_target="tpu_custom_call" | custom-call | tf_op jit(solution)/shard_map/hand_over/pallas_call | solution.py:582
